TPU v7x, 32 devices: a whole 2x2x4 slice. The times are simulated.
32 devices in a mesh: dp: 8 (over z, x), mp: 4 (over y, core).
Axes of the slice: x: 2, y: 2, z: 4, core: 2. Of those that a mesh axis runs over, the one named last changes fastest.
Arguments:
- tokens: bfloat16 [8, 2048, 1024], P('dp', 'mp'), may hold values from -6 to 6
- cotangent: bfloat16 [8, 2048, 1024], P('dp', 'mp'), may hold values from -6 to 6
- w_qkv: float32 [3, 1024, 1024], P(None, 'dp', 'mp'), may hold values from -0.1875 to 0.1875
- w_out: float32 [1024, 1024], P('mp', 'dp'), may hold values from -3 to 3
- w_up: float32 [1024, 4096], P('dp', 'mp'), may hold values from -0.1875 to 0.1875
- w_down: float32 [4096, 1024], P('mp', 'dp'), may hold values from -0.09375 to 0.09375
- gain_attn: float32 [1024], replicated, may hold values from 0.5 to 1.5
- shift_attn: float32 [1024], replicated, may hold values from -1.5 to 1.5
- gain_ffn: float32 [1024], replicated, may hold values from 0.5 to 1.5
- shift_ffn: float32 [1024], replicated, may hold values from -1.5 to 1.5
- bias_up: float32 [4096], P('mp'), may hold values from -1.5 to 1.5
- bias_down: float32 [1024], replicated, may hold values from -1.5 to 1.5
- random_blocks: int32 [8, 16, 30, 3], P('dp', 'mp'), may hold values from 1 to 30
Outputs:
- out_tokens: bfloat16 [8, 2048, 1024], P('dp', 'mp')
- grad_tokens: float32 [8, 2048, 1024], P('dp', 'mp')
- new_qkv: float32 [3, 1024, 1024], P(None, 'dp', 'mp')
- qkv_rows: float32 [3, 1024], P(None, 'dp')
- qkv_cols: float32 [3, 1024], P(None, 'mp')
- new_out: float32 [1024, 1024], P('mp', 'dp')
- out_rows: float32 [1024], P('mp')
- out_cols: float32 [1024], P('dp')
- new_up: float32 [1024, 4096], P('dp', 'mp')
- up_rows: float32 [1024], P('dp')
- up_cols: float32 [4096], P('mp')
- new_down: float32 [4096, 1024], P('mp', 'dp')
- down_rows: float32 [4096], P('mp')
- down_cols: float32 [1024], P('dp')
- grad_gain_attn: float32 [1024], replicated
- grad_shift_attn: float32 [1024], replicated
- grad_gain_ffn: float32 [1024], replicated
- grad_shift_ffn: float32 [1024], replicated
- grad_bias_up: float32 [4096], P('mp')
- grad_bias_down: float32 [1024], replicated
Inputs may be any that keep to these rules, and one draw needn't show every extreme that they name: `random_blocks`: every entry names a block of the same document other than its first and last; entries may repeat and may equal window blocks.
All inputs are finite; a program needn't handle non-finite values.
Results may differ from a plain program's by a relative error of at most 0.04.
Values may be sent and summed in bfloat16 or wider, within the bound.
No kernel may reach another device: no remote copies, remote signals or barrier semaphores. Data moves between devices by JAX's collectives and lax.ppermute only.
A program may use at most 192 MiB of HBM per device.

v0:
```python
import jax
import jax.numpy as jnp
from jax import lax
from jax.sharding import PartitionSpec as P

D = 1024
FF = 4096
BLOCK = 64
EPS_NORM = 1e-05
EPS_FACTOR = 1e-30
LEARN_RATE = 0.1
GELU_SCALE = 0.7978845608028654


def gelu_tanh(values):
    return (
        0.5 * values * (1.0 + jnp.tanh(GELU_SCALE * (values + 0.044715 * values * values * values)))
    )


def block_table(random_rows, blocks_all):
    middle = jnp.arange(1, blocks_all - 1, dtype=jnp.int32)[:, None]
    fixed = jnp.concatenate(
        [
            jnp.zeros_like(middle),
            middle - 1,
            middle,
            middle + 1,
            jnp.zeros_like(middle) + (blocks_all - 1),
        ],
        axis=1,
    )
    return jnp.concatenate([fixed, random_rows], axis=1)


def spread_rows(local_part):
    return lax.all_gather(local_part, "mp", axis=0, tiled=True)


def spread_grads(local_part):
    return lax.all_gather(local_part, "mp", axis=0, tiled=True)


def combine_heads(partial_value):
    return lax.psum_scatter(
        partial_value.astype(jnp.bfloat16), "mp", scatter_dimension=0, tiled=True
    ).astype(jnp.float32)


def combine_grads(partial_value):
    return lax.psum_scatter(
        partial_value.astype(jnp.bfloat16), "mp", scatter_dimension=0, tiled=True
    ).astype(jnp.float32)


def norm_forward(values, norm_gain, norm_shift):
    center = jnp.mean(values, axis=1, keepdims=True)
    spread = values - center
    variance = jnp.mean(spread * spread, axis=1, keepdims=True)
    inverse = lax.rsqrt(variance + EPS_NORM)
    normal = spread * inverse
    return ((normal * norm_gain + norm_shift).astype(jnp.bfloat16), normal, inverse)


def norm_backward(grad_norm, norm_gain, normal, inverse):
    scaled = grad_norm * norm_gain
    mean_plain = jnp.mean(scaled, axis=1, keepdims=True)
    mean_normal = jnp.mean(scaled * normal, axis=1, keepdims=True)
    grad_values = inverse * (scaled - mean_plain - normal * mean_normal)
    return (grad_values, jnp.sum(grad_norm * normal, axis=0), jnp.sum(grad_norm, axis=0))


def near_blocks(block_rows, key_table):
    return jnp.take(block_rows, key_table, axis=0).reshape(
        key_table.shape[0], -1, block_rows.shape[2]
    )


def attend_group(query_group, key_group, value_group, scaling):
    scores = (
        jnp.einsum("nqe,nke->nqk", query_group, key_group, preferred_element_type=jnp.float32)
        * scaling
    )
    highest = jnp.max(scores, axis=-1, keepdims=True)
    expanded = jnp.exp(scores - highest)
    summed = jnp.sum(expanded, axis=-1, keepdims=True)
    probs = (expanded / summed).astype(jnp.bfloat16)
    result = jnp.einsum("nqk,nke->nqe", probs, value_group, preferred_element_type=jnp.float32)
    return (result, highest + jnp.log(summed))


def attend_back(query_group, key_group, value_group, grad_group, log_total, scaling):
    scores = (
        jnp.einsum("nqe,nke->nqk", query_group, key_group, preferred_element_type=jnp.float32)
        * scaling
    )
    probs = jnp.exp(scores - log_total)
    grad_probs = jnp.einsum(
        "nqe,nke->nqk", grad_group, value_group, preferred_element_type=jnp.float32
    )
    center = jnp.sum(probs * grad_probs, axis=-1, keepdims=True)
    grad_score = (probs * (grad_probs - center)).astype(jnp.bfloat16)
    grad_query = (
        jnp.einsum("nqk,nke->nqe", grad_score, key_group, preferred_element_type=jnp.float32)
        * scaling
    )
    grad_key = (
        jnp.einsum("nqk,nqe->nke", grad_score, query_group, preferred_element_type=jnp.float32)
        * scaling
    )
    grad_value = jnp.einsum(
        "nqk,nqe->nke", probs.astype(jnp.bfloat16), grad_group, preferred_element_type=jnp.float32
    )
    return (grad_query, grad_key, grad_value)


def head_forward(queries, key_rows, value_rows, key_table):
    head_dim = queries.shape[1]
    blocks_all = queries.shape[0] // BLOCK
    scaling = head_dim ** (-0.5)
    query_blocks = queries.reshape(blocks_all, BLOCK, head_dim)
    key_near = near_blocks(key_rows.reshape(blocks_all, BLOCK, head_dim), key_table)
    value_near = near_blocks(value_rows.reshape(blocks_all, BLOCK, head_dim), key_table)
    out_mid, log_mid = attend_group(query_blocks[1:-1], key_near, value_near, scaling)
    query_ends = jnp.concatenate([query_blocks[0], query_blocks[-1]], axis=0)
    out_ends, log_ends = attend_group(query_ends[None], key_rows[None], value_rows[None], scaling)
    joined = jnp.concatenate([out_ends[:, :BLOCK], out_mid, out_ends[:, BLOCK:]], axis=0)
    return (joined.reshape(-1, head_dim).astype(jnp.bfloat16), log_mid, log_ends)


def head_backward(queries, key_rows, value_rows, key_table, grad_out, log_mid, log_ends):
    head_dim = queries.shape[1]
    blocks_all = queries.shape[0] // BLOCK
    scaling = head_dim ** (-0.5)
    query_blocks = queries.reshape(blocks_all, BLOCK, head_dim)
    grad_blocks = grad_out.reshape(blocks_all, BLOCK, head_dim)
    key_near = near_blocks(key_rows.reshape(blocks_all, BLOCK, head_dim), key_table)
    value_near = near_blocks(value_rows.reshape(blocks_all, BLOCK, head_dim), key_table)
    mid_query, mid_key, mid_value = attend_back(
        query_blocks[1:-1], key_near, value_near, grad_blocks[1:-1], log_mid, scaling
    )
    segment_ids = key_table.reshape(-1)
    key_sum = jax.ops.segment_sum(
        mid_key.reshape(-1, BLOCK, head_dim), segment_ids, num_segments=blocks_all
    ).reshape(-1, head_dim)
    value_sum = jax.ops.segment_sum(
        mid_value.reshape(-1, BLOCK, head_dim), segment_ids, num_segments=blocks_all
    ).reshape(-1, head_dim)
    query_ends = jnp.concatenate([query_blocks[0], query_blocks[-1]], axis=0)
    grad_ends = jnp.concatenate([grad_blocks[0], grad_blocks[-1]], axis=0)
    end_query, end_key, end_value = attend_back(
        query_ends[None], key_rows[None], value_rows[None], grad_ends[None], log_ends, scaling
    )
    grad_query = jnp.concatenate(
        [end_query[:, :BLOCK], mid_query, end_query[:, BLOCK:]], axis=0
    ).reshape(-1, head_dim)
    return (
        grad_query.astype(jnp.bfloat16),
        (key_sum + end_key[0]).astype(jnp.bfloat16),
        (value_sum + end_value[0]).astype(jnp.bfloat16),
    )


def factored(weight, gradient, row_sum, col_sum, whole_sum, row_total, col_total):
    row_mean = row_sum / col_total + EPS_FACTOR
    col_mean = col_sum / row_total + EPS_FACTOR
    whole = whole_sum / (row_total * col_total) + EPS_FACTOR
    row_factor = row_mean / whole[..., None]
    col_factor = col_mean / whole[..., None]
    update = gradient * lax.rsqrt(
        row_factor[..., :, None] * col_factor[..., None, :] * whole[..., None, None]
    )
    return (weight - LEARN_RATE * update, row_factor, col_factor)


def body(
    tokens,
    cotangent,
    w_qkv,
    w_out,
    w_up,
    w_down,
    gain_attn,
    shift_attn,
    gain_ffn,
    shift_ffn,
    bias_up,
    bias_down,
    random_blocks,
):
    qkv_low, out_low, up_low, down_low = (
        lax.all_gather(w_qkv.astype(jnp.bfloat16), "dp", axis=1, tiled=True),
        lax.all_gather(w_out.astype(jnp.bfloat16), "dp", axis=1, tiled=True),
        lax.all_gather(w_up.astype(jnp.bfloat16), "dp", axis=0, tiled=True),
        lax.all_gather(w_down.astype(jnp.bfloat16), "dp", axis=1, tiled=True),
    )
    local_heads = random_blocks.shape[1]
    head_dim = qkv_low.shape[2] // local_heads
    inputs = tokens[0].astype(jnp.float32)
    normed_low, normal_one, inverse_one = norm_forward(inputs, gain_attn, shift_attn)
    normed_full = spread_rows(normed_low)
    seq_rows = normed_full.shape[0]
    blocks_all = seq_rows // BLOCK
    tables = jax.vmap(lambda random_rows: block_table(random_rows, blocks_all))(random_blocks[0])
    project = jnp.einsum(
        "ld,cde->cle", normed_full, qkv_low, preferred_element_type=jnp.float32
    ).astype(jnp.bfloat16)
    heads_split = project.reshape(3, seq_rows, local_heads, head_dim).transpose(0, 2, 1, 3)
    attended, log_mid, log_ends = lax.map(
        lambda members: head_forward(*members),
        (heads_split[0], heads_split[1], heads_split[2], tables),
    )
    heads_out = attended.transpose(1, 0, 2).reshape(seq_rows, local_heads * head_dim)
    branch_part = jnp.dot(heads_out, out_low, preferred_element_type=jnp.float32)
    middle = inputs + combine_heads(branch_part)
    second_low, normal_two, inverse_two = norm_forward(middle, gain_ffn, shift_ffn)
    second_full = spread_rows(second_low)
    hidden_pre = jnp.dot(second_full, up_low, preferred_element_type=jnp.float32) + bias_up
    activated, gelu_pull = jax.vjp(gelu_tanh, hidden_pre)
    active_low = activated.astype(jnp.bfloat16)
    ffn_out = combine_heads(jnp.dot(active_low, down_low, preferred_element_type=jnp.float32))
    out_tokens = (middle + ffn_out + bias_down).astype(jnp.bfloat16)
    grad_top = cotangent[0]
    grad_top_full = spread_grads(grad_top)
    grad_down_w = jnp.einsum(
        "lf,ld->fd", active_low, grad_top_full, preferred_element_type=jnp.float32
    )
    grad_active = jnp.einsum(
        "ld,fd->lf", grad_top_full, down_low, preferred_element_type=jnp.float32
    )
    grad_hidden = gelu_pull(grad_active)[0].astype(jnp.bfloat16)
    grad_bias_up = jnp.sum(grad_hidden.astype(jnp.float32), axis=0)
    grad_up_w = jnp.einsum(
        "ld,lf->df", second_full, grad_hidden, preferred_element_type=jnp.float32
    )
    grad_second = combine_grads(
        jnp.einsum("lf,df->ld", grad_hidden, up_low, preferred_element_type=jnp.float32)
    )
    grad_middle_norm, grad_gain_ffn, grad_shift_ffn = norm_backward(
        grad_second, gain_ffn, normal_two, inverse_two
    )
    grad_top_float = grad_top.astype(jnp.float32)
    grad_middle = grad_top_float + grad_middle_norm
    grad_bias_down = jnp.sum(grad_top_float, axis=0)
    grad_branch_full = spread_grads(grad_middle.astype(jnp.bfloat16))
    grad_out_w = jnp.einsum(
        "la,ld->ad", heads_out, grad_branch_full, preferred_element_type=jnp.float32
    )
    grad_heads = jnp.einsum(
        "ld,ad->la", grad_branch_full, out_low, preferred_element_type=jnp.float32
    ).astype(jnp.bfloat16)
    grad_split = grad_heads.reshape(seq_rows, local_heads, head_dim).transpose(1, 0, 2)
    grad_query, grad_key, grad_value = lax.map(
        lambda members: head_backward(*members),
        (heads_split[0], heads_split[1], heads_split[2], tables, grad_split, log_mid, log_ends),
    )
    grad_project = (
        jnp.stack([grad_query, grad_key, grad_value])
        .transpose(0, 2, 1, 3)
        .reshape(3, seq_rows, local_heads * head_dim)
    )
    grad_qkv_w = jnp.einsum(
        "ld,cle->cde", normed_full, grad_project, preferred_element_type=jnp.float32
    )
    grad_normed = combine_grads(
        jnp.einsum("cle,cde->ld", grad_project, qkv_low, preferred_element_type=jnp.float32)
    )
    grad_input_norm, grad_gain_attn, grad_shift_attn = norm_backward(
        grad_normed, gain_attn, normal_one, inverse_one
    )
    grad_tokens = (grad_middle + grad_input_norm)[None]
    shard_qkv, shard_out, shard_up, shard_down = (
        lax.psum_scatter(
            grad_qkv_w.astype(jnp.bfloat16), "dp", scatter_dimension=1, tiled=True
        ).astype(jnp.float32),
        lax.psum_scatter(
            grad_out_w.astype(jnp.bfloat16), "dp", scatter_dimension=1, tiled=True
        ).astype(jnp.float32),
        lax.psum_scatter(
            grad_up_w.astype(jnp.bfloat16), "dp", scatter_dimension=0, tiled=True
        ).astype(jnp.float32),
        lax.psum_scatter(
            grad_down_w.astype(jnp.bfloat16), "dp", scatter_dimension=1, tiled=True
        ).astype(jnp.float32),
    )
    square_qkv = shard_qkv * shard_qkv
    square_out = shard_out * shard_out
    square_up = shard_up * shard_up
    square_down = shard_down * shard_down
    mp_terms = (
        jnp.sum(square_qkv, axis=2),
        jnp.sum(square_out, axis=0),
        jnp.sum(square_up, axis=1),
        jnp.sum(square_down, axis=0),
    )
    dp_terms = (
        jnp.sum(square_qkv, axis=1),
        jnp.sum(square_out, axis=1),
        jnp.sum(square_up, axis=0),
        jnp.sum(square_down, axis=1),
    )
    token_grads = (grad_gain_attn, grad_shift_attn, grad_gain_ffn, grad_shift_ffn, grad_bias_down)
    local_totals = (
        jnp.sum(square_qkv, axis=(1, 2)),
        jnp.sum(square_out),
        jnp.sum(square_up),
        jnp.sum(square_down),
    )
    mp_input = mp_terms + token_grads
    mp_sums = tuple(lax.psum(mp_input, "mp"))
    dp_input = dp_terms + mp_sums[4:9] + (grad_bias_up,)
    dp_sums = tuple(lax.psum(dp_input, "dp"))
    totals = tuple(
        lax.psum((local_totals[0], local_totals[1], local_totals[2], local_totals[3]), ("dp", "mp"))
    )
    new_qkv, qkv_rows, qkv_cols = factored(
        w_qkv, shard_qkv, mp_sums[0], dp_sums[0], totals[0], D, D
    )
    new_out, out_rows, out_cols = factored(
        w_out, shard_out, dp_sums[1], mp_sums[1], totals[1], D, D
    )
    new_up, up_rows, up_cols = factored(w_up, shard_up, mp_sums[2], dp_sums[2], totals[2], D, FF)
    new_down, down_rows, down_cols = factored(
        w_down, shard_down, dp_sums[3], mp_sums[3], totals[3], FF, D
    )
    return (
        out_tokens[None],
        grad_tokens,
        new_qkv,
        qkv_rows,
        qkv_cols,
        new_out,
        out_rows,
        out_cols,
        new_up,
        up_rows,
        up_cols,
        new_down,
        down_rows,
        down_cols,
        dp_sums[4],
        dp_sums[5],
        dp_sums[6],
        dp_sums[7],
        dp_sums[9],
        dp_sums[8],
    )


def solution(mesh):
    placed = (
        P("dp", "mp", None),
        P("dp", "mp", None),
        P(None, "dp", "mp"),
        P("mp", "dp"),
        P("dp", "mp"),
        P("mp", "dp"),
        P(),
        P(),
        P(),
        P(),
        P("mp"),
        P(),
        P("dp", "mp", None, None),
    )
    return jax.shard_map(
        body,
        mesh=mesh,
        in_specs=placed,
        out_specs=(
            P("dp", "mp", None),
            P("dp", "mp", None),
            P(None, "dp", "mp"),
            P(None, "dp"),
            P(None, "mp"),
            P("mp", "dp"),
            P("mp"),
            P("dp"),
            P("dp", "mp"),
            P("dp"),
            P("mp"),
            P("mp", "dp"),
            P("mp"),
            P("dp"),
            P(),
            P(),
            P(),
            P(),
            P("mp"),
            P(),
        ),
        check_vma=False,
    )
```

profile of v0, /device:TPU:0, one launch (start us, length us, event | category | flops | bytes accessed | tf_op | source)
XLA Modules:
  0.0 1205.3 jit_solution(2356265805523504589)
XLA Ops:
  15.6 31.7 %all_gather.26 = bf16[256,1024]{1,0:T(8,128)(2,1)S(1)} all-gather(bf16[256,128]{1,0:T(8,128)(2,1)S(1)} %convert_element_type.165), channel_id=1, replica_groups=mesh['dp'=8,'mp'=4] {'dp'}, dimensions={1}, use_global_device_ids=true | all-gather | bytes 589824 | tf_op jit(solution)/shard_map/all_gather | solution.py:193
  47.2 15.1 %all-gather.11.cloned.1.call-done = bf16[3,1024,256]{1,2,0:T(8,128)(2,1)} async-done(((bf16[3,128,256]{1,2,0:T(8,128)(2,1)}), bf16[3,1024,256]{1,2,0:T(8,128)(2,1)}) %all-gather.11.cloned.1.call-update) | async-done | bytes 1572880 | tf_op jit(solution)/shard_map/all_gather | solution.py:192
  62.3 35.4 %all-gather.9.cloned.1.call-done = bf16[2048,1024]{1,0:T(8,128)(2,1)} async-done(((bf16[512,1024]{1,0:T(8,128)(2,1)}), bf16[2048,1024]{1,0:T(8,128)(2,1)}) %all-gather.9.cloned.1.call-update) | async-done | bytes 4194320 | tf_op jit(solution)/shard_map/all_gather | solution.py:37
  97.8 7.8 fusion.54
  119.0 85.0 %while.28 = (s32[]{:T(128)}, bf16[4,2048,64]{1,2,0:T(8,128)(2,1)}, f32[4,30,64,1]{2,1,3,0:T(8,128)}, f32[4,1,128,1]{2,3,1,0:T(1,128)}, bf16[4,2048,64]{2,1,0:T(8...) while((s32[]{:T(128)}, bf16[4,2048,64]{1,2,0:T(8,128)(2,1)}, ...), condition=%wide.region_7.9_spmd, body=%wide.region_2.8_spmd.sunk | while | flops 331841952 | bytes 38948568 | solution.py:209
  210.3 42.8 %reduce-scatter.15.cloned.1.call-done = bf16[512,1024]{1,0:T(8,128)(2,1)} async-done(((bf16[2048,1024]{1,0:T(8,128)(2,1)}), bf16[512,1024]{1,0:T(8,128)(2,1)}) %reduce-scatter.15.cloned.1.call-update) | async-done | bytes 1048592 | tf_op jit(solution)/shard_map/reduce_scatter | solution.py:45
  259.7 8.7 reduce-scatter.19.cloned.1.call-start
  268.4 36.3 %all-gather.15.cloned.1.call-done = bf16[1024,1024]{1,0:T(8,128)(2,1)} async-done(((bf16[128,1024]{1,0:T(8,128)(2,1)}), bf16[1024,1024]{1,0:T(8,128)(2,1)}) %all-gather.15.cloned.1.call-update) | async-done | bytes 2097168 | tf_op jit(solution)/shard_map/all_gather | solution.py:194
  304.7 35.1 %all-gather.13.cloned.1.call-done = bf16[2048,1024]{1,0:T(8,128)(2,1)} async-done(((bf16[512,1024]{1,0:T(8,128)(2,1)}), bf16[2048,1024]{1,0:T(8,128)(2,1)}) %all-gather.13.cloned.1.call-update) | async-done | bytes 4194320 | tf_op jit(solution)/shard_map/all_gather | solution.py:37
  339.7 10.6 fusion.121
  350.4 43.2 %all-gather.17.cloned.1.call-done = bf16[1024,1024]{1,0:T(8,128)(2,1)} async-done(((bf16[1024,128]{1,0:T(8,128)(2,1)}), bf16[1024,1024]{1,0:T(8,128)(2,1)}) %all-gather.17.cloned.1.call-update) | async-done | bytes 2097168 | tf_op jit(solution)/shard_map/all_gather | solution.py:195
  393.5 34.3 %all-gather.21.cloned.1.call-done = bf16[1,2048,1024]{2,1,0:T(8,128)(2,1)} async-done(((bf16[1,512,1024]{2,1,0:T(8,128)(2,1)}), bf16[1,2048,1024]{2,1,0:T(8,128)(2,1)}) %all-gather.21.cloned.1.call-update) | async-done | bytes 4194320 | tf_op jit(solution)/shard_map/all_gather | solution.py:41
  427.9 15.6 %convert_reduce_fusion = (f32[1024]{0:T(1024)}, bf16[2048,1024]{1,0:T(8,128)(2,1)S(1)}) fusion(bf16[1024,1024]{1,0:T(8,128)(2,1)} %all-gather.17.cloned.1.call-done, bf16[1,2048,1024]{2,1,0:T(8,128)(2,1)} %all-gather.21.cloned.1.call-done, f32[2048,1024]{1,0:T(8,128)} %fusion.121, f32[1024]{0:T(1024)S(1)} %copy-done.59), kind=kOutput, calls=%fused_computation.108 | convolution fusion | flops 4351589376 | bytes 18882560 | tf_op jit(solution)/shard_map/ld,fd->lf/dot_general | solution.py:228
  452.3 44.2 %reduce-scatter.19.cloned.1.call-done = bf16[512,1024]{1,0:T(8,128)(2,1)} async-done(((bf16[2048,1024]{1,0:T(8,128)(2,1)}), bf16[512,1024]{1,0:T(8,128)(2,1)}) %reduce-scatter.19.cloned.1.call-update) | async-done | bytes 1048592 | tf_op jit(solution)/shard_map/reduce_scatter | solution.py:51
  503.9 10.6 fusion.85
  517.2 9.5 convolution_convert_fusion.5
  526.8 11.7 all-gather.19.cloned.1.call-done
  547.1 391.1 %while.29 = (s32[]{:T(128)}, bf16[4,2048,64]{1,2,0:T(8,128)(2,1)}, bf16[4,2048,64]{1,2,0:T(8,128)(2,1)}, bf16[4,2048,64]{1,2,0:T(8,128)(2,1)}, bf16[4,2048,64]{2...) while((s32[]{:T(128)}, bf16[4,2048,64]{1,2,0:T(8,128)(2,1)}, ...), condition=%wide.region_20.22_spmd, body=%wide.region_15.21_spmd.sunk | while | flops 817038464 | bytes 143667312 | solution.py:253
  585.8 25.0 %scatter_fusion.1 = f32[32,64,64]{2,1,0:T(8,128)S(1)} fusion(f32[32,64,64]{2,1,0:T(8,128)S(1)} %broadcast.323.clone.1, s32[240]{0:T(256)S(1)} %copy-done.34, f32[240,64,64]{2,1,0:T(8,128)} %bitcast.349), kind=kCustom, calls=%fused_computation.5.clone.1 | custom fusion | flops 983040 | bytes 11797440 | tf_op jit(solution)/shard_map/while/body/eval_jaxpr/scatter-add | solution.py:146
  618.8 24.9 %scatter_fusion = f32[32,64,64]{2,1,0:T(8,128)S(1)} fusion(f32[32,64,64]{2,1,0:T(8,128)S(1)} %broadcast.323.clone, s32[240]{0:T(256)S(1)} %copy-done.34, f32[240,64,64]{2,1,0:T(8,128)} %bitcast.350), kind=kCustom, calls=%fused_computation.4.clone.1 | custom fusion | flops 983040 | bytes 11797440 | tf_op jit(solution)/shard_map/while/body/eval_jaxpr/scatter-add | solution.py:143
  683.6 24.9 %scatter_fusion.1 = f32[32,64,64]{2,1,0:T(8,128)S(1)} fusion(f32[32,64,64]{2,1,0:T(8,128)S(1)} %broadcast.323.clone.1, s32[240]{0:T(256)S(1)} %copy-done.34, f32[240,64,64]{2,1,0:T(8,128)} %bitcast.349), kind=kCustom, calls=%fused_computation.5.clone.1 | custom fusion | flops 983040 | bytes 11797440 | tf_op jit(solution)/shard_map/while/body/eval_jaxpr/scatter-add | solution.py:146
  716.6 24.9 %scatter_fusion = f32[32,64,64]{2,1,0:T(8,128)S(1)} fusion(f32[32,64,64]{2,1,0:T(8,128)S(1)} %broadcast.323.clone, s32[240]{0:T(256)S(1)} %copy-done.34, f32[240,64,64]{2,1,0:T(8,128)} %bitcast.350), kind=kCustom, calls=%fused_computation.4.clone.1 | custom fusion | flops 983040 | bytes 11797440 | tf_op jit(solution)/shard_map/while/body/eval_jaxpr/scatter-add | solution.py:143
  781.3 24.9 %scatter_fusion.1 = f32[32,64,64]{2,1,0:T(8,128)S(1)} fusion(f32[32,64,64]{2,1,0:T(8,128)S(1)} %broadcast.323.clone.1, s32[240]{0:T(256)S(1)} %copy-done.34, f32[240,64,64]{2,1,0:T(8,128)} %bitcast.349), kind=kCustom, calls=%fused_computation.5.clone.1 | custom fusion | flops 983040 | bytes 11797440 | tf_op jit(solution)/shard_map/while/body/eval_jaxpr/scatter-add | solution.py:146
  814.2 24.9 %scatter_fusion = f32[32,64,64]{2,1,0:T(8,128)S(1)} fusion(f32[32,64,64]{2,1,0:T(8,128)S(1)} %broadcast.323.clone, s32[240]{0:T(256)S(1)} %copy-done.34, f32[240,64,64]{2,1,0:T(8,128)} %bitcast.350), kind=kCustom, calls=%fused_computation.4.clone.1 | custom fusion | flops 983040 | bytes 11797440 | tf_op jit(solution)/shard_map/while/body/eval_jaxpr/scatter-add | solution.py:143
  879.0 24.9 %scatter_fusion.1 = f32[32,64,64]{2,1,0:T(8,128)S(1)} fusion(f32[32,64,64]{2,1,0:T(8,128)S(1)} %broadcast.323.clone.1, s32[240]{0:T(256)S(1)} %copy-done.34, f32[240,64,64]{2,1,0:T(8,128)} %bitcast.349), kind=kCustom, calls=%fused_computation.5.clone.1 | custom fusion | flops 983040 | bytes 11797440 | tf_op jit(solution)/shard_map/while/body/eval_jaxpr/scatter-add | solution.py:146
  911.9 24.9 %scatter_fusion = f32[32,64,64]{2,1,0:T(8,128)S(1)} fusion(f32[32,64,64]{2,1,0:T(8,128)S(1)} %broadcast.323.clone, s32[240]{0:T(256)S(1)} %copy-done.34, f32[240,64,64]{2,1,0:T(8,128)} %bitcast.350), kind=kCustom, calls=%fused_computation.4.clone.1 | custom fusion | flops 983040 | bytes 11797440 | tf_op jit(solution)/shard_map/while/body/eval_jaxpr/scatter-add | solution.py:143
  966.8 11.1 convolution_convert_fusion.3
  983.7 23.4 %reduce-scatter.27.cloned.1.call-done = bf16[128,256]{1,0:T(8,128)(2,1)} async-done(((bf16[1024,256]{1,0:T(8,128)(2,1)}), bf16[128,256]{1,0:T(8,128)(2,1)}) %reduce-scatter.27.cloned.1.call-update) | async-done | bytes 65552
  1008.7 66.7 %reduce-scatter.25.cloned.1.call-done = bf16[128,768]{1,0:T(8,128)(2,1)} async-done(((bf16[1024,768]{1,0:T(8,128)(2,1)}), bf16[128,768]{1,0:T(8,128)(2,1)}) %reduce-scatter.25.cloned.1.call-update) | async-done | bytes 196624
  1080.8 40.3 %all-reduce = (f32[3]{0:T(128)}, f32[]{:T(128)}, f32[]{:T(128)}, f32[]{:T(128)}) all-reduce(f32[3]{0:T(128)} %get-tuple-element.246, f32[]{:T(128)} %get-tuple-element.249, f32[]{:T(128)} %get-tuple-element.243, f32[]{:T(128)} %get-tuple-element.240), channel_id=1, replica_groups=mesh['dp'=8,'mp'=4] {'dp','mp'}, use_global_device_ids=true, to_apply=%region_28.30 | all-reduce | flops 6 | bytes 48 | tf_op jit(solution)/shard_map/psum | solution.py:314
  1127.1 11.7 all-reduce.2
  1138.8 37.6 %all-reduce.1 = (f32[3,256]{1,0:T(4,128)}, f32[256]{0:T(256)}, f32[1024]{0:T(1024)}, f32[1024]{0:T(1024)}, f32[1024]{0:T(1024)}, /*index=5*/f32[1024]{0:T(1024)}...) all-reduce(f32[3,256]{1,0:T(4,128)} %get-tuple-element.247, ...), channel_id=1, replica_groups=mesh['dp'=8,'mp'=4] {'dp'}, use_global_device_ids=true, to_apply=%region_30.32 | all-reduce | flops 9216 | bytes 73728 | tf_op jit(solution)/shard_map/psum | solution.py:312
  (564 shorter events, 404.3 us)
Async XLA Ops:
  7.2 55.1 %all-gather.11.cloned.1.call-start = ((), (), s32[]{:S(2)}) async-start(), calls=%async_computation.9 | async-start | bytes 1769472 | tf_op jit(solution)/shard_map/all_gather | solution.py:192
  8.5 97.1 %copy-start.22 = (f32[3,128,256]{1,2,0:T(8,128)}, f32[3,128,256]{1,2,0:T(8,128)S(1)}, u32[]{:S(2)}) copy-start(f32[3,128,256]{1,2,0:T(8,128)S(1)} %copy.97) | copy-start | bytes 1179652
  9.3 88.5 %all-gather.9.cloned.1.call-start = ((), (), s32[]{:S(2)}) async-start(), calls=%async_computation.8 | async-start | bytes 5242880 | tf_op jit(solution)/shard_map/all_gather | solution.py:37
  14.6 238.5 %reduce-scatter.15.cloned.1.call-start = ((), (), s32[]{:S(2)}) async-start(), calls=%async_computation.10 | async-start | bytes 5242880 | tf_op jit(solution)/shard_map/reduce_scatter | solution.py:45
  47.2 156.7 %copy-start.26 = (bf16[256,1024]{1,0:T(8,128)(2,1)}, bf16[256,1024]{1,0:T(8,128)(2,1)S(1)}, u32[]{:S(2)}) copy-start(bf16[256,1024]{1,0:T(8,128)(2,1)S(1)} %all_gather.26) | copy-start | bytes 1572868
  208.4 48.1 %copy-start.37 = (f32[1024]{0:T(1024)S(1)}, f32[1024]{0:T(1024)}, u32[]{:S(2)}) copy-start(f32[1024]{0:T(1024)} %param.27) | copy-start | bytes 12292
  208.4 48.1 %copy-start.51 = (f32[1024]{0:T(1024)S(1)}, f32[1024]{0:T(1024)}, u32[]{:S(2)}) copy-start(f32[1024]{0:T(1024)} %param.28) | copy-start | bytes 12292
  208.5 96.2 %all-gather.15.cloned.1.call-start = ((), (), s32[]{:S(2)}) async-start(), calls=%async_computation.12 | async-start | bytes 2359296 | tf_op jit(solution)/shard_map/all_gather | solution.py:194
  210.3 129.5 %all-gather.13.cloned.1.call-start = ((), (), s32[]{:S(2)}) async-start(), calls=%async_computation.11 | async-start | bytes 5242880 | tf_op jit(solution)/shard_map/all_gather | solution.py:37
  254.8 244.6 %copy-start.35 = (f32[512]{0:T(512)}, f32[512]{0:T(512)S(1)}, u32[]{:S(2)}) copy-start(f32[512]{0:T(512)S(1)} %broadcast_multiply_fusion.4) | copy-start | bytes 6148
  256.6 242.8 %copy-start.39 = (f32[512]{0:T(512)}, f32[512]{0:T(512)S(1)}, u32[]{:S(2)}) copy-start(f32[512]{0:T(512)S(1)} %add_rsqrt_fusion) | copy-start | bytes 6148
  258.1 135.4 %all-gather.17.cloned.1.call-start = ((), (), s32[]{:S(2)}) async-start(), calls=%async_computation.13 | async-start | bytes 2359296 | tf_op jit(solution)/shard_map/all_gather | solution.py:195
  258.9 168.9 %all-gather.21.cloned.1.call-start = ((), (), s32[]{:S(2)}) async-start(), calls=%async_computation.19 | async-start | bytes 5242880 | tf_op jit(solution)/shard_map/all_gather | solution.py:41
  259.7 168.2 %copy-start.59 = (f32[1024]{0:T(1024)S(1)}, f32[1024]{0:T(1024)}, u32[]{:S(2)}) copy-start(f32[1024]{0:T(1024)} %param.29) | copy-start | bytes 12292
  259.7 236.8 %reduce-scatter.19.cloned.1.call-start = ((), (), s32[]{:S(2)}) async-start(), calls=%async_computation.15 | async-start | bytes 5242880 | tf_op jit(solution)/shard_map/reduce_scatter | solution.py:51
  451.8 48.8 %copy-start.9 = (bf16[1,512,1024]{2,1,0:T(8,128)(2,1)S(1)}, bf16[1,512,1024]{2,1,0:T(8,128)(2,1)}, u32[]{:S(2)}) copy-start(bf16[1,512,1024]{2,1,0:T(8,128)(2,1)} %param.20) | copy-start | bytes 3145732
  451.8 86.7 %all-gather.19.cloned.1.call-start = ((), (), s32[]{:S(2)}) async-start(), calls=%async_computation.16 | async-start | bytes 5242880 | tf_op jit(solution)/shard_map/all_gather | solution.py:41
  503.8 476.1 %reduce-scatter.29.cloned.1.call-start = ((), (), s32[]{:S(2)}) async-start(), calls=%async_computation.22 | async-start | bytes 2359296
  517.1 464.8 %reduce-scatter.23.cloned.1.call-start = ((), (), s32[]{:S(2)}) async-start(), calls=%async_computation.18 | async-start | bytes 2359296 | tf_op jit(solution)/shard_map/reduce_scatter | solution.py:279
  526.7 480.4 %reduce-scatter.27.cloned.1.call-start = ((), (), s32[]{:S(2)}) async-start(), calls=%async_computation.21 | async-start | bytes 589824
  945.1 130.3 %reduce-scatter.25.cloned.1.call-start = ((), (), s32[]{:S(2)}) async-start(), calls=%async_computation.20 | async-start | bytes 1769472
  957.4 166.9 %reduce-scatter.21.cloned.1.call-start = ((), (), s32[]{:S(2)}) async-start(), calls=%async_computation.17 | async-start | bytes 5242880 | tf_op jit(solution)/shard_map/reduce_scatter | solution.py:51
  965.3 228.4 %reduce-scatter.17.cloned.1.call-start = ((), (), s32[]{:S(2)}) async-start(), calls=%async_computation.14 | async-start | bytes 5242880 | tf_op jit(solution)/shard_map/reduce_scatter | solution.py:45
  978.0 146.3 %copy-start.6 = (bf16[1,512,1024]{2,1,0:T(8,128)(2,1)S(1)}, bf16[1,512,1024]{2,1,0:T(8,128)(2,1)}, u32[]{:S(2)}) copy-start(bf16[1,512,1024]{2,1,0:T(8,128)(2,1)} %param.19) | copy-start | bytes 3145732
  978.0 146.3 %copy-start.42 = (f32[512]{0:T(512)S(1)}, f32[512]{0:T(512)}, u32[]{:S(2)}) copy-start(f32[512]{0:T(512)} %copy-done.41) | copy-start | bytes 6148
  978.0 200.6 %copy-start.23 = (f32[3,128,256]{1,2,0:T(8,128)S(1)}, f32[3,128,256]{1,2,0:T(8,128)}, u32[]{:S(2)}) copy-start(f32[3,128,256]{1,2,0:T(8,128)} %copy-done.22) | copy-start | bytes 1179652
  981.1 94.3 %copy-start.25 = (bf16[1024,128]{1,0:T(8,128)(2,1)}, bf16[1024,128]{1,0:T(8,128)(2,1)S(1)}, u32[]{:S(2)}) copy-start(bf16[1024,128]{1,0:T(8,128)(2,1)S(1)} %copy.129) | copy-start | bytes 786436
  1008.0 67.4 %copy-start.32 = (bf16[256,128]{1,0:T(8,128)(2,1)}, bf16[256,128]{1,0:T(8,128)(2,1)S(1)}, u32[]{:S(2)}) copy-start(bf16[256,128]{1,0:T(8,128)(2,1)S(1)} %copy.127) | copy-start | bytes 196612
  1077.1 116.5 %copy-start.8 = (bf16[512,1024]{1,0:T(8,128)(2,1)S(1)}, bf16[512,1024]{1,0:T(8,128)(2,1)}, u32[]{:S(2)}) copy-start(bf16[512,1024]{1,0:T(8,128)(2,1)} %reduce-scatter.15.cloned.1.call-done) | copy-start | bytes 3145732
  1077.1 116.5 %copy-start.36 = (f32[512]{0:T(512)S(1)}, f32[512]{0:T(512)}, u32[]{:S(2)}) copy-start(f32[512]{0:T(512)} %copy-done.35) | copy-start | bytes 6148
  1077.1 116.5 %copy-start.38 = (f32[1024]{0:T(1024)S(1)}, f32[1024]{0:T(1024)}, u32[]{:S(2)}) copy-start(f32[1024]{0:T(1024)} %param.27) | copy-start | bytes 12292
  1077.1 116.5 %copy-start.40 = (f32[512]{0:T(512)S(1)}, f32[512]{0:T(512)}, u32[]{:S(2)}) copy-start(f32[512]{0:T(512)} %copy-done.39) | copy-start | bytes 6148
  (93 other events, 862.0 us)
Sparse Core Ops, SparseCore 0:
  10.7 51.6 all-gather.10
  64.5 33.2 all-gather.8
  208.6 44.5 reduce-scatter.14
  255.3 49.2 all-gather.14
  306.7 32.9 all-gather.12
  342.4 51.0 all-gather.16
  395.1 32.6 all-gather.20
  451.9 44.4 reduce-scatter.18
  504.0 34.4 all-gather.18
  541.9 67.8 reduce-scatter.28
  613.3 66.8 reduce-scatter.22
  945.2 61.8 reduce-scatter.26
  1011.5 63.8 reduce-scatter.24
  1077.8 43.9 reduce-scatter.20
  1124.4 44.6 reduce-scatter.16
where the time goes:
time: 1220 us; the launch traced here: 1210 us
  waiting for transfers between devices  389 us (32%)
  other arithmetic  303 us (25%)
  local copies, waits for them, and re-layouts  189 us (15%)
  matrix products  175 us (14%)
  blocking collectives  121 us (10%)
  between operations  16.9 us (1%)
    scatter-add x4, other arithmetic, head_backward(): jax.ops.segment_sum(mid_value.reshape(-1, BLOCK, head_dim), segment_ids,...  99.5 us
    scatter-add x4, other arithmetic, head_backward(): jax.ops.segment_sum(mid_key.reshape(-1, BLOCK, head_dim), segment_ids, nu...  99.5 us
    unnamed x18, waiting for transfers between devices  91 us
    all_gather x2, waiting for transfers between devices, spread_rows(): return lax.all_gather(local_part, 'mp', axis=0, tiled=True)  70.5 us
    gather x16, local copies, waits for them, and re-layouts, near_blocks(): jnp.take(block_rows, key_table, axis=0)  47.5 us
    all_gather x2, waiting for transfers between devices, spread_grads(): return lax.all_gather(local_part, 'mp', axis=0, tiled=True)  46 us
    reduce_scatter x2, waiting for transfers between devices, combine_grads(): lax.psum_scatter(partial_value.astype(jnp.bfloat16), 'mp', scatter_dimens...  44.2 us
    all_gather x1, waiting for transfers between devices, body(): lax.all_gather(w_down.astype(jnp.bfloat16), 'dp', axis=1, tiled=True)  43.2 us
  transfers between devices with their start and end apart: 15, of which 11 were waited for; matrix products, arithmetic and copies ran while one was open for 42% of the time, Pallas kernels for 0%

commit v1 on v0

--- a/solution.py
+++ b/solution.py
@@ -10,6 +10,28 @@
 EPS_FACTOR = 1e-30
 LEARN_RATE = 0.1
 GELU_SCALE = 0.7978845608028654
+
+
+def joined_along(blocks, dim):
+    blocks = jnp.moveaxis(blocks, 0, dim)
+    shape = blocks.shape
+    return blocks.reshape(*shape[:dim], shape[dim] * shape[dim + 1], *shape[dim + 2 :])
+
+
+def collect(x, axis, dim):
+    count = lax.axis_size(axis)
+    pairs = [(i, (i + 1) % count) for i in range(count)]
+    back = [(b, a) for a, b in pairs]
+    lower, upper = ([], [])
+    for step in range(count - 1):
+        if step % 2 == 0:
+            lower.append(lax.ppermute(lower[-1] if lower else x, axis, pairs))
+        else:
+            upper.append(lax.ppermute(upper[-1] if upper else x, axis, back))
+    tiles = jnp.stack([*lower[::-1], x, *upper])
+    shift = lax.axis_index(axis) - len(lower)
+    tiles = tiles[(jnp.arange(count) - shift) % count]
+    return joined_along(tiles, dim)
 
 
 def gelu_tanh(values):
@@ -191,7 +213,7 @@
     qkv_low, out_low, up_low, down_low = (
         lax.all_gather(w_qkv.astype(jnp.bfloat16), "dp", axis=1, tiled=True),
         lax.all_gather(w_out.astype(jnp.bfloat16), "dp", axis=1, tiled=True),
-        lax.all_gather(w_up.astype(jnp.bfloat16), "dp", axis=0, tiled=True),
+        collect(w_up.astype(jnp.bfloat16), "dp", 0),
         lax.all_gather(w_down.astype(jnp.bfloat16), "dp", axis=1, tiled=True),
     )
     local_heads = random_blocks.shape[1]

time: 1220 us -> 1180 us (0.967)
  waiting for transfers between devices: 389 us -> 316 us
  starting transfers between devices: 9.9 us -> 27.6 us
    all_gather x1 -> x0, waiting for transfers between devices: 36.3 us -> none  [body(): lax.all_gather(w_up.astype(jnp.bfloat16), 'dp', axis=0, tiled=True)]
    all_gather x2, waiting for transfers between devices: 70.5 us -> 35.4 us  [spread_rows(): return lax.all_gather(local_part, 'mp', axis=0, tiled=True)]
    ppermute x0 -> x7, starting transfers between devices: none -> 26.2 us  [the longest x3 19.6 us: collect(): upper.append(lax.ppermute(upper[-1] if upper else x, axis, back))]
    all_gather x1, waiting for transfers between devices: 43.2 us -> 17.4 us  [body(): lax.all_gather(w_down.astype(jnp.bfloat16), 'dp', axis=1, tiled=True)]
    ppermute x0 -> x7, waiting for transfers between devices: none -> 23 us  [the longest x4 23 us: collect(): lower.append(lax.ppermute(lower[-1] if lower else x, axis, pairs))]
    unnamed x103 -> x109, local copies, waits for them, and re-layouts: 28.1 us -> 33.3 us
    unnamed x18 -> x17, waiting for transfers between devices: 91 us -> 90.6 us
  transfers between devices with their start and end apart: 15 -> 21, of which waited for: 11 -> 13; matrix products, arithmetic and copies ran while one was open for 42% -> 45% of each run, Pallas kernels for 0% -> 0%
where the time goes in v1:
time: 1180 us; the launch traced here: 1160 us
  waiting for transfers between devices  316 us (27%)
  other arithmetic  303 us (26%)
  local copies, waits for them, and re-layouts  199 us (17%)
  matrix products  175 us (15%)
  blocking collectives  121 us (10%)
  starting transfers between devices  27.6 us (2%)
  between operations  16.7 us (1%)
    scatter-add x4, other arithmetic, head_backward(): jax.ops.segment_sum(mid_value.reshape(-1, BLOCK, head_dim), segment_ids,...  99.5 us
    scatter-add x4, other arithmetic, head_backward(): jax.ops.segment_sum(mid_key.reshape(-1, BLOCK, head_dim), segment_ids, nu...  99.5 us
    unnamed x17, waiting for transfers between devices  90.6 us
    gather x16, local copies, waits for them, and re-layouts, near_blocks(): jnp.take(block_rows, key_table, axis=0)  47.4 us
    all_gather x2, waiting for transfers between devices, spread_grads(): return lax.all_gather(local_part, 'mp', axis=0, tiled=True)  45.7 us
    reduce_scatter x2, waiting for transfers between devices, combine_grads(): lax.psum_scatter(partial_value.astype(jnp.bfloat16), 'mp', scatter_dimens...  44.6 us
    reduce_scatter x2, waiting for transfers between devices, combine_heads(): lax.psum_scatter(partial_value.astype(jnp.bfloat16), 'mp', scatter_dimens...  44.2 us
    psum x1, blocking collectives, body(): lax.psum((local_totals[0], local_totals[1], local_totals[2], local_totals...  40.3 us
  transfers between devices with their start and end apart: 21, of which 13 were waited for; matrix products, arithmetic and copies ran while one was open for 45% of the time, Pallas kernels for 0%

profile of v1, /device:TPU:0, one launch (start us, length us, event | category | flops | bytes accessed | tf_op | source)
XLA Modules:
  0.0 1159.9 jit_solution(3016615629254987378)
XLA Ops:
  15.6 31.7 %all_gather.23 = bf16[256,1024]{1,0:T(8,128)(2,1)S(1)} all-gather(bf16[256,128]{1,0:T(8,128)(2,1)S(1)} %convert_element_type.165), channel_id=1, replica_groups=mesh['dp'=8,'mp'=4] {'dp'}, dimensions={1}, use_global_device_ids=true | all-gather | bytes 589824 | tf_op jit(solution)/shard_map/all_gather | solution.py:215
  47.2 15.1 %all-gather.10.cloned.1.call-done = bf16[3,1024,256]{1,2,0:T(8,128)(2,1)} async-done(((bf16[3,128,256]{1,2,0:T(8,128)(2,1)}), bf16[3,1024,256]{1,2,0:T(8,128)(2,1)}) %all-gather.10.cloned.1.call-update) | async-done | bytes 1572880 | tf_op jit(solution)/shard_map/all_gather | solution.py:214
  62.4 35.4 %all-gather.8.cloned.1.call-done = bf16[2048,1024]{1,0:T(8,128)(2,1)} async-done(((bf16[512,1024]{1,0:T(8,128)(2,1)}), bf16[2048,1024]{1,0:T(8,128)(2,1)}) %all-gather.8.cloned.1.call-update) | async-done | bytes 4194320 | tf_op jit(solution)/shard_map/all_gather | solution.py:59
  97.8 7.8 fusion.54
  119.0 85.0 %while.28 = (s32[]{:T(128)}, bf16[4,2048,64]{1,2,0:T(8,128)(2,1)}, f32[4,30,64,1]{2,1,3,0:T(8,128)}, f32[4,1,128,1]{2,3,1,0:T(1,128)}, bf16[4,2048,64]{2,1,0:T(8...) while((s32[]{:T(128)}, bf16[4,2048,64]{1,2,0:T(8,128)(2,1)}, ...), condition=%wide.region_7.9_spmd, body=%wide.region_2.8_spmd.sunk | while | flops 331841952 | bytes 38948568 | solution.py:231
  209.0 44.2 %reduce-scatter.15.cloned.1.call-done = bf16[512,1024]{1,0:T(8,128)(2,1)} async-done(((bf16[2048,1024]{1,0:T(8,128)(2,1)}), bf16[512,1024]{1,0:T(8,128)(2,1)}) %reduce-scatter.15.cloned.1.call-update) | async-done | bytes 1048592 | tf_op jit(solution)/shard_map/reduce_scatter | solution.py:67
  261.2 9.3 collective-permute-done
  296.1 8.1 collective-permute-start.6
  321.3 10.6 fusion.123
  331.9 17.4 %all-gather.14.cloned.1.call-done = bf16[1024,1024]{1,0:T(8,128)(2,1)} async-done(((bf16[1024,128]{1,0:T(8,128)(2,1)}), bf16[1024,1024]{1,0:T(8,128)(2,1)}) %all-gather.14.cloned.1.call-update) | async-done | bytes 2097168 | tf_op jit(solution)/shard_map/all_gather | solution.py:217
  349.3 34.2 %all-gather.18.cloned.1.call-done = bf16[1,2048,1024]{2,1,0:T(8,128)(2,1)} async-done(((bf16[1,512,1024]{2,1,0:T(8,128)(2,1)}), bf16[1,2048,1024]{2,1,0:T(8,128)(2,1)}) %all-gather.18.cloned.1.call-update) | async-done | bytes 4194320 | tf_op jit(solution)/shard_map/all_gather | solution.py:63
  383.5 15.8 %convert_reduce_fusion = (f32[1024]{0:T(1024)}, bf16[2048,1024]{1,0:T(8,128)(2,1)S(1)}) fusion(bf16[1024,1024]{1,0:T(8,128)(2,1)} %all-gather.14.cloned.1.call-done, bf16[1,2048,1024]{2,1,0:T(8,128)(2,1)} %all-gather.18.cloned.1.call-done, f32[2048,1024]{1,0:T(8,128)} %fusion.123, f32[1024]{0:T(1024)S(1)} %copy-done.59), kind=kOutput, calls=%fused_computation.109 | convolution fusion | flops 4351589376 | bytes 18882560 | tf_op jit(solution)/shard_map/ld,fd->lf/dot_general | solution.py:250
  407.6 44.6 %reduce-scatter.19.cloned.1.call-done = bf16[512,1024]{1,0:T(8,128)(2,1)} async-done(((bf16[2048,1024]{1,0:T(8,128)(2,1)}), bf16[512,1024]{1,0:T(8,128)(2,1)}) %reduce-scatter.19.cloned.1.call-update) | async-done | bytes 1048592 | tf_op jit(solution)/shard_map/reduce_scatter | solution.py:73
  458.7 10.6 fusion.85
  472.1 9.4 convolution_convert_fusion.5
  481.6 11.5 all-gather.16.cloned.1.call-done
  502.2 391.1 %while.29 = (s32[]{:T(128)}, bf16[4,2048,64]{1,2,0:T(8,128)(2,1)}, bf16[4,2048,64]{1,2,0:T(8,128)(2,1)}, bf16[4,2048,64]{1,2,0:T(8,128)(2,1)}, bf16[4,2048,64]{2...) while((s32[]{:T(128)}, bf16[4,2048,64]{1,2,0:T(8,128)(2,1)}, ...), condition=%wide.region_20.22_spmd, body=%wide.region_15.21_spmd.sunk | while | flops 817038464 | bytes 143667312 | solution.py:275
  540.8 25.0 %scatter_fusion.1 = f32[32,64,64]{2,1,0:T(8,128)S(1)} fusion(f32[32,64,64]{2,1,0:T(8,128)S(1)} %broadcast.392.clone.1, s32[240]{0:T(256)S(1)} %copy-done.35, f32[240,64,64]{2,1,0:T(8,128)} %bitcast.368), kind=kCustom, calls=%fused_computation.6.clone.1 | custom fusion | flops 983040 | bytes 11797440 | tf_op jit(solution)/shard_map/while/body/eval_jaxpr/scatter-add | solution.py:168
  573.9 24.9 %scatter_fusion = f32[32,64,64]{2,1,0:T(8,128)S(1)} fusion(f32[32,64,64]{2,1,0:T(8,128)S(1)} %broadcast.392.clone, s32[240]{0:T(256)S(1)} %copy-done.35, f32[240,64,64]{2,1,0:T(8,128)} %bitcast.369), kind=kCustom, calls=%fused_computation.5.clone.1 | custom fusion | flops 983040 | bytes 11797440 | tf_op jit(solution)/shard_map/while/body/eval_jaxpr/scatter-add | solution.py:165
  638.6 24.9 %scatter_fusion.1 = f32[32,64,64]{2,1,0:T(8,128)S(1)} fusion(f32[32,64,64]{2,1,0:T(8,128)S(1)} %broadcast.392.clone.1, s32[240]{0:T(256)S(1)} %copy-done.35, f32[240,64,64]{2,1,0:T(8,128)} %bitcast.368), kind=kCustom, calls=%fused_computation.6.clone.1 | custom fusion | flops 983040 | bytes 11797440 | tf_op jit(solution)/shard_map/while/body/eval_jaxpr/scatter-add | solution.py:168
  671.6 24.9 %scatter_fusion = f32[32,64,64]{2,1,0:T(8,128)S(1)} fusion(f32[32,64,64]{2,1,0:T(8,128)S(1)} %broadcast.392.clone, s32[240]{0:T(256)S(1)} %copy-done.35, f32[240,64,64]{2,1,0:T(8,128)} %bitcast.369), kind=kCustom, calls=%fused_computation.5.clone.1 | custom fusion | flops 983040 | bytes 11797440 | tf_op jit(solution)/shard_map/while/body/eval_jaxpr/scatter-add | solution.py:165
  736.3 24.9 %scatter_fusion.1 = f32[32,64,64]{2,1,0:T(8,128)S(1)} fusion(f32[32,64,64]{2,1,0:T(8,128)S(1)} %broadcast.392.clone.1, s32[240]{0:T(256)S(1)} %copy-done.35, f32[240,64,64]{2,1,0:T(8,128)} %bitcast.368), kind=kCustom, calls=%fused_computation.6.clone.1 | custom fusion | flops 983040 | bytes 11797440 | tf_op jit(solution)/shard_map/while/body/eval_jaxpr/scatter-add | solution.py:168
  769.3 24.9 %scatter_fusion = f32[32,64,64]{2,1,0:T(8,128)S(1)} fusion(f32[32,64,64]{2,1,0:T(8,128)S(1)} %broadcast.392.clone, s32[240]{0:T(256)S(1)} %copy-done.35, f32[240,64,64]{2,1,0:T(8,128)} %bitcast.369), kind=kCustom, calls=%fused_computation.5.clone.1 | custom fusion | flops 983040 | bytes 11797440 | tf_op jit(solution)/shard_map/while/body/eval_jaxpr/scatter-add | solution.py:165
  833.9 24.9 %scatter_fusion.1 = f32[32,64,64]{2,1,0:T(8,128)S(1)} fusion(f32[32,64,64]{2,1,0:T(8,128)S(1)} %broadcast.392.clone.1, s32[240]{0:T(256)S(1)} %copy-done.35, f32[240,64,64]{2,1,0:T(8,128)} %bitcast.368), kind=kCustom, calls=%fused_computation.6.clone.1 | custom fusion | flops 983040 | bytes 11797440 | tf_op jit(solution)/shard_map/while/body/eval_jaxpr/scatter-add | solution.py:168
  866.9 24.9 %scatter_fusion = f32[32,64,64]{2,1,0:T(8,128)S(1)} fusion(f32[32,64,64]{2,1,0:T(8,128)S(1)} %broadcast.392.clone, s32[240]{0:T(256)S(1)} %copy-done.35, f32[240,64,64]{2,1,0:T(8,128)} %bitcast.369), kind=kCustom, calls=%fused_computation.5.clone.1 | custom fusion | flops 983040 | bytes 11797440 | tf_op jit(solution)/shard_map/while/body/eval_jaxpr/scatter-add | solution.py:165
  912.5 7.8 bitcast_convert_fusion
  921.8 11.1 convolution_convert_fusion.3
  938.7 23.3 %reduce-scatter.27.cloned.1.call-done = bf16[128,256]{1,0:T(8,128)(2,1)} async-done(((bf16[1024,256]{1,0:T(8,128)(2,1)}), bf16[128,256]{1,0:T(8,128)(2,1)}) %reduce-scatter.27.cloned.1.call-update) | async-done | bytes 65552
  963.7 66.5 %reduce-scatter.25.cloned.1.call-done = bf16[128,768]{1,0:T(8,128)(2,1)} async-done(((bf16[1024,768]{1,0:T(8,128)(2,1)}), bf16[128,768]{1,0:T(8,128)(2,1)}) %reduce-scatter.25.cloned.1.call-update) | async-done | bytes 196624
  1035.6 40.3 %all-reduce = (f32[3]{0:T(128)}, f32[]{:T(128)}, f32[]{:T(128)}, f32[]{:T(128)}) all-reduce(f32[3]{0:T(128)} %get-tuple-element.246, f32[]{:T(128)} %get-tuple-element.249, f32[]{:T(128)} %get-tuple-element.243, f32[]{:T(128)} %get-tuple-element.240), channel_id=1, replica_groups=mesh['dp'=8,'mp'=4] {'dp','mp'}, use_global_device_ids=true, to_apply=%region_28.30 | all-reduce | flops 6 | bytes 48 | tf_op jit(solution)/shard_map/psum | solution.py:336
  1081.9 11.8 %all-reduce.2 = (f32[1024]{0:T(1024)}, f32[1024]{0:T(1024)}, f32[1024]{0:T(1024)}, f32[1024]{0:T(1024)}, f32[1024]{0:T(1024)}, /*index=5*/f32[3,128]{1,0:T(4,128)}, f32[128]{0:T(128)}, f32[128]{0:T(128)}, f32[128]{0:T(128)}) all-reduce(f32[1024]{0:T(1024)} %get-tuple-element.233, ...), channel_id=1, replica_groups=mesh['dp'=8,'mp'=4] {'mp'}, use_global_device_ids=true, to_apply=%region_53.55 | all-reduce | flops 5888 | bytes 47104 | tf_op jit(solution)/shard_map/psum | solution.py:332
  1093.6 37.6 %all-reduce.1 = (f32[3,256]{1,0:T(4,128)}, f32[256]{0:T(256)}, f32[1024]{0:T(1024)}, f32[1024]{0:T(1024)}, f32[1024]{0:T(1024)}, /*index=5*/f32[1024]{0:T(1024)}...) all-reduce(f32[3,256]{1,0:T(4,128)} %get-tuple-element.247, ...), channel_id=1, replica_groups=mesh['dp'=8,'mp'=4] {'dp'}, use_global_device_ids=true, to_apply=%region_30.32 | all-reduce | flops 9216 | bytes 73728 | tf_op jit(solution)/shard_map/psum | solution.py:334
  (586 shorter events, 438.3 us)
Async XLA Ops:
  7.2 55.2 %all-gather.10.cloned.1.call-start = ((), (), s32[]{:S(2)}) async-start(), calls=%async_computation.9 | async-start | bytes 1769472 | tf_op jit(solution)/shard_map/all_gather | solution.py:214
  8.5 97.1 %copy-start.23 = (f32[3,128,256]{1,2,0:T(8,128)}, f32[3,128,256]{1,2,0:T(8,128)S(1)}, u32[]{:S(2)}) copy-start(f32[3,128,256]{1,2,0:T(8,128)S(1)} %copy.97) | copy-start | bytes 1179652
  9.3 88.5 %all-gather.8.cloned.1.call-start = ((), (), s32[]{:S(2)}) async-start(), calls=%async_computation.8 | async-start | bytes 5242880 | tf_op jit(solution)/shard_map/all_gather | solution.py:59
  14.6 238.6 %reduce-scatter.15.cloned.1.call-start = ((), (), s32[]{:S(2)}) async-start(), calls=%async_computation.10 | async-start | bytes 5242880 | tf_op jit(solution)/shard_map/reduce_scatter | solution.py:67
  47.2 156.8 %copy-start.27 = (bf16[256,1024]{1,0:T(8,128)(2,1)}, bf16[256,1024]{1,0:T(8,128)(2,1)S(1)}, u32[]{:S(2)}) copy-start(bf16[256,1024]{1,0:T(8,128)(2,1)S(1)} %all_gather.23) | copy-start | bytes 1572868
  208.5 112.8 %all-gather.12.cloned.1.call-start = ((), (), s32[]{:S(2)}) async-start(), calls=%async_computation.11 | async-start | bytes 5242880 | tf_op jit(solution)/shard_map/all_gather | solution.py:59
  254.8 200.4 %copy-start.36 = (f32[512]{0:T(512)}, f32[512]{0:T(512)S(1)}, u32[]{:S(2)}) copy-start(f32[512]{0:T(512)S(1)} %broadcast_multiply_fusion.4) | copy-start | bytes 6148
  256.7 198.5 %copy-start.40 = (f32[512]{0:T(512)}, f32[512]{0:T(512)S(1)}, u32[]{:S(2)}) copy-start(f32[512]{0:T(512)S(1)} %add_rsqrt_fusion) | copy-start | bytes 6148
  258.2 91.1 %all-gather.14.cloned.1.call-start = ((), (), s32[]{:S(2)}) async-start(), calls=%async_computation.12 | async-start | bytes 2359296 | tf_op jit(solution)/shard_map/all_gather | solution.py:217
  259.0 124.5 %all-gather.18.cloned.1.call-start = ((), (), s32[]{:S(2)}) async-start(), calls=%async_computation.18 | async-start | bytes 5242880 | tf_op jit(solution)/shard_map/all_gather | solution.py:63
  259.6 192.6 %reduce-scatter.19.cloned.1.call-start = ((), (), s32[]{:S(2)}) async-start(), calls=%async_computation.14 | async-start | bytes 5242880 | tf_op jit(solution)/shard_map/reduce_scatter | solution.py:73
  259.7 10.8 collective-permute-start
  270.5 10.6 collective-permute-start.1
  270.5 13.1 %collective-permute-start.4 = (bf16[128,1024]{1,0:T(8,128)(2,1)S(1)}, bf16[128,1024]{1,0:T(8,128)(2,1)S(1)}, u32[]{:S(2)}, u32[]{:S(2)}) collective-permute-start(bf16[128,1024]{1,0:T(8,128)(2,1)S(1)} %convert_element_type.169), channel_id=1, source_target_pairs={{4,0},{8,4},{12,8},{16,12},{20,16},{24,20},{28,24},{0,28},{5,1},{9... | collective-permute-start | bytes 786440 | tf_op jit(solution)/shard_map/ppermute | solution.py:30
  281.1 12.4 %collective-permute-start.2 = (bf16[128,1024]{1,0:T(8,128)(2,1)S(1)}, bf16[128,1024]{1,0:T(8,128)(2,1)}, u32[]{:S(2)}, u32[]{:S(2)}) collective-permute-start(bf16[128,1024]{1,0:T(8,128)(2,1)S(1)} %collective-permute-done.1), channel_id=1, source_target_pairs={{0,4},{4,8},{8,12},{12,16},{16,20},{20,24},{24,28},{28,0},{1,5},{5... | collective-permute-start | bytes 786440 | tf_op jit(solution)/shard_map/ppermute | solution.py:28
  283.6 12.5 %collective-permute-start.5 = (bf16[128,1024]{1,0:T(8,128)(2,1)S(1)}, bf16[128,1024]{1,0:T(8,128)(2,1)}, u32[]{:S(2)}, u32[]{:S(2)}) collective-permute-start(bf16[128,1024]{1,0:T(8,128)(2,1)S(1)} %collective-permute-done.4), channel_id=1, source_target_pairs={{4,0},{8,4},{12,8},{16,12},{20,16},{24,20},{28,24},{0,28},{5,1},{9... | collective-permute-start | bytes 786440 | tf_op jit(solution)/shard_map/ppermute | solution.py:30
  293.5 15.5 %collective-permute-start.3 = (bf16[128,1024]{1,0:T(8,128)(2,1)}, bf16[128,1024]{1,0:T(8,128)(2,1)}, u32[]{:S(2)}, u32[]{:S(2)}) collective-permute-start(bf16[128,1024]{1,0:T(8,128)(2,1)} %collective-permute-done.2), channel_id=1, source_target_pairs={{0,4},{4,8},{8,12},{12,16},{16,20},{20,24},{24,28},{28,0},{1,5},{5... | collective-permute-start | bytes 786440 | tf_op jit(solution)/shard_map/ppermute | solution.py:28
  296.1 20.8 %collective-permute-start.6 = (bf16[128,1024]{1,0:T(8,128)(2,1)}, bf16[128,1024]{1,0:T(8,128)(2,1)S(1)}, u32[]{:S(2)}, u32[]{:S(2)}) collective-permute-start(bf16[128,1024]{1,0:T(8,128)(2,1)} %collective-permute-done.5), channel_id=1, source_target_pairs={{4,0},{8,4},{12,8},{16,12},{20,16},{24,20},{28,24},{0,28},{5,1},{9... | collective-permute-start | bytes 786440 | tf_op jit(solution)/shard_map/ppermute | solution.py:30
  407.6 85.6 %all-gather.16.cloned.1.call-start = ((), (), s32[]{:S(2)}) async-start(), calls=%async_computation.15 | async-start | bytes 5242880 | tf_op jit(solution)/shard_map/all_gather | solution.py:63
  458.5 476.5 %reduce-scatter.29.cloned.1.call-start = ((), (), s32[]{:S(2)}) async-start(), calls=%async_computation.21 | async-start | bytes 2359296
  472.1 464.9 %reduce-scatter.23.cloned.1.call-start = ((), (), s32[]{:S(2)}) async-start(), calls=%async_computation.17 | async-start | bytes 2359296 | tf_op jit(solution)/shard_map/reduce_scatter | solution.py:301
  481.6 480.5 %reduce-scatter.27.cloned.1.call-start = ((), (), s32[]{:S(2)}) async-start(), calls=%async_computation.20 | async-start | bytes 589824
  900.1 130.2 %reduce-scatter.25.cloned.1.call-start = ((), (), s32[]{:S(2)}) async-start(), calls=%async_computation.19 | async-start | bytes 1769472
  912.4 166.6 %reduce-scatter.21.cloned.1.call-start = ((), (), s32[]{:S(2)}) async-start(), calls=%async_computation.16 | async-start | bytes 5242880 | tf_op jit(solution)/shard_map/reduce_scatter | solution.py:73
  920.3 228.2 %reduce-scatter.17.cloned.1.call-start = ((), (), s32[]{:S(2)}) async-start(), calls=%async_computation.13 | async-start | bytes 5242880 | tf_op jit(solution)/shard_map/reduce_scatter | solution.py:67
  933.0 146.0 %copy-start.6 = (bf16[1,512,1024]{2,1,0:T(8,128)(2,1)S(1)}, bf16[1,512,1024]{2,1,0:T(8,128)(2,1)}, u32[]{:S(2)}) copy-start(bf16[1,512,1024]{2,1,0:T(8,128)(2,1)} %param.19) | copy-start | bytes 3145732
  933.0 146.0 %copy-start.43 = (f32[512]{0:T(512)S(1)}, f32[512]{0:T(512)}, u32[]{:S(2)}) copy-start(f32[512]{0:T(512)} %copy-done.42) | copy-start | bytes 6148
  933.0 200.4 %copy-start.24 = (f32[3,128,256]{1,2,0:T(8,128)S(1)}, f32[3,128,256]{1,2,0:T(8,128)}, u32[]{:S(2)}) copy-start(f32[3,128,256]{1,2,0:T(8,128)} %copy-done.23) | copy-start | bytes 1179652
  1031.9 116.5 %copy-start.8 = (bf16[512,1024]{1,0:T(8,128)(2,1)S(1)}, bf16[512,1024]{1,0:T(8,128)(2,1)}, u32[]{:S(2)}) copy-start(bf16[512,1024]{1,0:T(8,128)(2,1)} %reduce-scatter.15.cloned.1.call-done) | copy-start | bytes 3145732
  1031.9 116.5 %copy-start.37 = (f32[512]{0:T(512)S(1)}, f32[512]{0:T(512)}, u32[]{:S(2)}) copy-start(f32[512]{0:T(512)} %copy-done.36) | copy-start | bytes 6148
  1031.9 116.5 %copy-start.39 = (f32[1024]{0:T(1024)S(1)}, f32[1024]{0:T(1024)}, u32[]{:S(2)}) copy-start(f32[1024]{0:T(1024)} %param.27) | copy-start | bytes 12292
  1032.0 116.5 %copy-start.41 = (f32[512]{0:T(512)S(1)}, f32[512]{0:T(512)}, u32[]{:S(2)}) copy-start(f32[512]{0:T(512)} %copy-done.40) | copy-start | bytes 6148
  (99 other events, 1261.9 us)
Sparse Core Ops, SparseCore 0:
  10.7 51.6 all-gather.9
  64.5 33.2 all-gather.7
  208.6 44.5 reduce-scatter.14
  258.4 34.4 all-gather.11
  295.5 53.7 all-gather.13
  350.8 32.6 all-gather.17
  407.7 44.5 reduce-scatter.18
  458.6 34.4 all-gather.15
  496.7 67.9 reduce-scatter.28
  568.1 66.8 reduce-scatter.22
  900.2 61.8 reduce-scatter.26
  966.3 63.8 reduce-scatter.24
  1032.8 44.0 reduce-scatter.20
  1079.4 44.5 reduce-scatter.16
